TPU v7x, 512 devices: a whole 4x4x16 slice. The times are simulated.
512 devices in a mesh: span: 16 (over x, z_hi, core), seq: 32 (over y, z_lo).
Axes of the slice: x: 4, y: 4, z: 16 (z_hi: 2, z_lo: 8; z = z_hi * 8 + z_lo), core: 2. Of those that a mesh axis runs over, the one named last changes fastest.
Arguments:
- queries: bfloat16 [16, 1024, 4096], P('span', 'seq')
- keys: bfloat16 [16, 1024, 4096], P('span', 'seq')
- values: bfloat16 [16, 1024, 4096], P('span', 'seq'), may hold values from -6 to 6
- lengths: int32 [16], replicated, may hold values from 256 to 1024, as said below
- span_mask: int32 [16, 2], replicated, may hold values from 0 to 1, as said below
- levels: int32 [16], replicated, may hold values from 0 to 15, each once
- level_gain: float32 [16, 4096], replicated, may hold values from 0.1 to 1.9
Outputs:
- attended: bfloat16 [16, 1024, 4096], P('span', 'seq')
Inputs may be any that keep to these rules, and one draw needn't show every extreme that they name: `lengths`: each span has at least 256 live tokens; some span has all 1024. `span_mask`: entries with c - 1 - j < 0 are 0.
All inputs are finite; a program needn't handle non-finite values.
Results may differ from a plain program's by a relative error of at most 0.0047.
Values may be sent and summed in bfloat16 or wider, within the bound.
A program may use at most 64 MiB of HBM per device.

v0:
```python
import jax
import jax.numpy as jnp
from jax import lax
from jax.sharding import PartitionSpec as P

HD = 128
WIN = 2


def shifted(value, axis, steps):
    count = lax.axis_size(axis)
    leading, last = (max(0, -steps), min(count, count - steps))
    return lax.ppermute(value, axis, [(source, source + steps) for source in range(leading, last)])


def pick_entry(table, index):
    spots = jnp.arange(table.shape[0], dtype=jnp.int32)
    return jnp.sum(jnp.where(spots == index, table, 0))


def per_device(queries, keys, values, lengths, span_mask, levels, level_gain):
    span_count = lengths.shape[0]
    here = lax.axis_index("span")
    member = lax.axis_index("seq")
    moved_keys = []
    moved_values = []
    for step in range(1, WIN + 1):
        got_keys, got_values = shifted((keys, values), "span", step)
        moved_keys.append(got_keys)
        moved_values.append(got_values)
    earlier_keys = jnp.concatenate(moved_keys, 0)
    earlier_values = jnp.concatenate(moved_values, 0)
    query_heads, key_heads, value_heads, earlier_keys, earlier_values = (
        lax.all_to_all(queries, "seq", split_axis=2, concat_axis=1, tiled=True),
        lax.all_to_all(keys, "seq", split_axis=2, concat_axis=1, tiled=True),
        lax.all_to_all(values, "seq", split_axis=2, concat_axis=1, tiled=True),
        lax.all_to_all(earlier_keys, "seq", split_axis=2, concat_axis=1, tiled=True),
        lax.all_to_all(earlier_values, "seq", split_axis=2, concat_axis=1, tiled=True),
    )
    slot_count = query_heads.shape[1]
    width = query_heads.shape[2]
    heads_here = width // HD
    query_block = query_heads.reshape(slot_count, heads_here, HD)
    key_all = jnp.concatenate([key_heads, earlier_keys], 0).reshape(
        (WIN + 1) * slot_count, heads_here, HD
    )
    value_all = jnp.concatenate([value_heads, earlier_values], 0).reshape(
        (WIN + 1) * slot_count, heads_here, HD
    )
    slots = jnp.arange(slot_count, dtype=jnp.int32)
    row_select = jnp.arange(span_count, dtype=jnp.int32) == here
    mask_row = jnp.sum(jnp.where(row_select[:, None], span_mask, 0), 0)
    valid_parts = []
    for step in range(WIN + 1):
        live = slots < pick_entry(lengths, here - step)
        if step > 0:
            live = live & (here - step >= 0) & (mask_row[step - 1] == 1)
        valid_parts.append(live)
    valid = jnp.concatenate(valid_parts, 0)
    scale = 1.0 / jnp.sqrt(jnp.float32(HD))
    scores = (
        jnp.einsum("qhd,khd->hqk", query_block, key_all, preferred_element_type=jnp.float32) * scale
    )
    scores = jnp.where(valid[None, None, :], scores, jnp.float32(-1e30))
    top = jnp.max(scores, axis=-1, keepdims=True)
    expd = jnp.where(valid[None, None, :], jnp.exp(scores - top), jnp.float32(0.0))
    total = jnp.sum(expd, axis=-1)
    probs = expd.astype(jnp.bfloat16)
    summed = jnp.einsum("hqk,khd->qhd", probs, value_all, preferred_element_type=jnp.float32)
    mixed = summed / jnp.transpose(total)[:, :, None]
    level_here = pick_entry(levels, here)
    level_select = jnp.arange(span_count, dtype=jnp.int32) == level_here
    gain_full = jnp.sum(jnp.where(level_select[:, None], level_gain, jnp.float32(0.0)), 0)
    gain_here = lax.dynamic_slice_in_dim(gain_full, member * width, width, 0).reshape(
        heads_here, HD
    )
    gated = (mixed * gain_here[None, :, :]).astype(jnp.bfloat16).reshape(1, slot_count, width)
    return lax.all_to_all(gated, "seq", split_axis=1, concat_axis=2, tiled=True)


def solution(mesh):
    placed = (
        P("span", "seq", None),
        P("span", "seq", None),
        P("span", "seq", None),
        P(),
        P(),
        P(),
        P(),
    )
    return jax.shard_map(
        per_device, mesh=mesh, in_specs=placed, out_specs=P("span", "seq", None), check_vma=False
    )
```

profile of v0, /device:TPU:6, one launch (start us, length us, event | category | flops | bytes accessed | tf_op | source)
XLA Modules:
  0.0 344.2 jit_solution(2163153997473547255)
XLA Ops:
  0.0 4.5 %copy.48 = bf16[1,32,4096]{1,0,2:T(2,128)(2,1)S(1)} copy(bf16[1,32,4096]{2,1,0:T(8,128)(2,1)} %param.7) | data formatting | bytes 524288 | tf_op args[0]
  5.0 22.4 %reduce.8 = bf16[4096,32]{1,0:T(8,128)(2,1)S(1)} reduce(bf16[4096,1,32]{2,1,0:T(2,128)(2,1)S(1)} %bitcast.84, bf16[]{:T(256)} %broadcast.62), dimensions={1}, to_apply=%bitcast.66.reduce_sub_computation | reduce | bytes 524290
  27.4 1.7 reshape.69
  29.2 15.7 %all-to-all-start.4 = ((bf16[32,2,2048]{2,1,0:T(2,128)(2,1)}), bf16[32,2,2048]{2,1,0:T(2,128)(2,1)S(1)}, u32[]{:S(2)}, u32[]{:S(2)}) async-start(bf16[32,2,2048]{2,1,0:T(2,128)(2,1)} %reshape.69), calls=%async_computation.4 | async-start | bytes 524288 | tf_op jit(solution)/shard_map/all_to_all | solution.py:34
  44.9 4.5 %copy.42 = bf16[1,32,4096]{1,0,2:T(2,128)(2,1)S(1)} copy(bf16[1,32,4096]{2,1,0:T(8,128)(2,1)} %param.8) | data formatting | bytes 524288 | tf_op args[1]
  49.4 22.4 %reduce.7 = bf16[4096,32]{1,0:T(8,128)(2,1)S(1)} reduce(bf16[4096,1,32]{2,1,0:T(2,128)(2,1)S(1)} %bitcast.85, bf16[]{:T(256)} %broadcast.62), dimensions={1}, to_apply=%bitcast.64.reduce_sub_computation | reduce | bytes 524290
  71.8 1.7 reshape.67
  73.5 12.7 %all-to-all-start.2 = ((bf16[32,2,2048]{2,1,0:T(2,128)(2,1)}), bf16[32,2,2048]{2,1,0:T(2,128)(2,1)}, u32[]{:S(2)}, u32[]{:S(2)}) async-start(bf16[32,2,2048]{2,1,0:T(2,128)(2,1)} %reshape.67), calls=%async_computation.2 | async-start | bytes 524288 | tf_op jit(solution)/shard_map/all_to_all | solution.py:35
  86.2 4.5 %copy.36 = bf16[1,32,4096]{1,0,2:T(2,128)(2,1)S(1)} copy(bf16[1,32,4096]{2,1,0:T(8,128)(2,1)} %param.9) | data formatting | bytes 524288 | tf_op args[2]
  90.7 22.4 %reduce.6 = bf16[4096,32]{1,0:T(8,128)(2,1)S(1)} reduce(bf16[4096,1,32]{2,1,0:T(2,128)(2,1)S(1)} %bitcast.86, bf16[]{:T(256)} %broadcast.62), dimensions={1}, to_apply=%bitcast.60.reduce_sub_computation | reduce | bytes 524290
  113.1 1.7 reshape.63
  114.9 12.2 %all-to-all-start = ((bf16[32,2,2048]{2,1,0:T(2,128)(2,1)}), bf16[32,2,2048]{2,1,0:T(2,128)(2,1)S(1)}, u32[]{:S(2)}, u32[]{:S(2)}) async-start(bf16[32,2,2048]{2,1,0:T(2,128)(2,1)} %reshape.63), calls=%async_computation | async-start | bytes 524288 | tf_op jit(solution)/shard_map/all_to_all | solution.py:36
  127.1 8.2 %collective-permute-start.1 = (bf16[1,32,4096]{2,1,0:T(8,128)(2,1)}, bf16[1,32,4096]{2,1,0:T(8,128)(2,1)S(1)}, u32[]{:S(2)}, u32[]{:S(2)}) collective-permute-start(bf16[1,32,4096]{2,1,0:T(8,128)(2,1)} %param.9), channel_id=1, source_target_pairs={{0,64},{32,96},{64,128},{96,160},{128,192},{160,224},{192,256},{22... | collective-permute-start | bytes 786440 | tf_op jit(solution)/shard_map/ppermute | solution.py:13
  135.3 1.9 collective-permute-start
  137.2 8.4 %collective-permute-done.1 = bf16[1,32,4096]{2,1,0:T(8,128)(2,1)S(1)} collective-permute-done((bf16[1,32,4096]{2,1,0:T(8,128)(2,1)}, bf16[1,32,4096]{2,1,0:T(8,128)(2,1)S(1)}, u32[]{:S(2)}, u32[]{:S(2)}) %collective-permute-start.1) | collective-permute-done | bytes 262176 | tf_op jit(solution)/shard_map/ppermute | solution.py:13
  145.6 10.4 %collective-permute-done = bf16[1,32,4096]{2,1,0:T(8,128)(2,1)S(1)} collective-permute-done((bf16[1,32,4096]{2,1,0:T(8,128)(2,1)}, bf16[1,32,4096]{2,1,0:T(8,128)(2,1)S(1)}, u32[]{:S(2)}, u32[]{:S(2)}) %collective-permute-start) | collective-permute-done | bytes 262176 | tf_op jit(solution)/shard_map/ppermute | solution.py:13
  156.0 2.8 copy.39
  158.8 2.7 reshape.61
  161.5 31.7 %all-to-all-start.1 = ((bf16[32,2,4096]{2,1,0:T(2,128)(2,1)}), bf16[32,2,4096]{2,1,0:T(2,128)(2,1)S(1)}, u32[]{:S(2)}, u32[]{:S(2)}) async-start(bf16[32,2,4096]{2,1,0:T(2,128)(2,1)} %reshape.61), calls=%async_computation.1 | async-start | bytes 1048576 | tf_op jit(solution)/shard_map/all_to_all | solution.py:38
  193.2 5.3 %collective-permute-start.3 = (bf16[1,32,4096]{2,1,0:T(8,128)(2,1)}, bf16[1,32,4096]{2,1,0:T(8,128)(2,1)S(1)}, u32[]{:S(2)}, u32[]{:S(2)}) collective-permute-start(bf16[1,32,4096]{2,1,0:T(8,128)(2,1)} %param.8), channel_id=1, source_target_pairs={{0,64},{32,96},{64,128},{96,160},{128,192},{160,224},{192,256},{22... | collective-permute-start | bytes 786440 | tf_op jit(solution)/shard_map/ppermute | solution.py:13
  198.6 1.9 collective-permute-start.2
  200.5 11.7 %collective-permute-done.3 = bf16[1,32,4096]{2,1,0:T(8,128)(2,1)S(1)} collective-permute-done((bf16[1,32,4096]{2,1,0:T(8,128)(2,1)}, bf16[1,32,4096]{2,1,0:T(8,128)(2,1)S(1)}, u32[]{:S(2)}, u32[]{:S(2)}) %collective-permute-start.3) | collective-permute-done | bytes 262176 | tf_op jit(solution)/shard_map/ppermute | solution.py:13
  212.2 4.9 %collective-permute-done.2 = bf16[1,32,4096]{2,1,0:T(8,128)(2,1)S(1)} collective-permute-done((bf16[1,32,4096]{2,1,0:T(8,128)(2,1)}, bf16[1,32,4096]{2,1,0:T(8,128)(2,1)S(1)}, u32[]{:S(2)}, u32[]{:S(2)}) %collective-permute-start.2) | collective-permute-done | bytes 262176 | tf_op jit(solution)/shard_map/ppermute | solution.py:13
  217.2 2.8 copy.45
  219.9 2.7 reshape.65
  222.6 6.3 %all-to-all-done.1 = bf16[32,2,4096]{2,1,0:T(2,128)(2,1)S(1)} async-done(((bf16[32,2,4096]{2,1,0:T(2,128)(2,1)}), bf16[32,2,4096]{2,1,0:T(2,128)(2,1)S(1)}, u32[]{:S(2)}, u32[]{:S(2)}) %all-to-all-start.1) | async-done | bytes 524320 | tf_op jit(solution)/shard_map/all_to_all | solution.py:38
  229.0 36.7 %all-to-all-start.3 = ((bf16[32,2,4096]{2,1,0:T(2,128)(2,1)}), bf16[32,2,4096]{2,1,0:T(2,128)(2,1)S(1)}, u32[]{:S(2)}, u32[]{:S(2)}) async-start(bf16[32,2,4096]{2,1,0:T(2,128)(2,1)} %reshape.65), calls=%async_computation.3 | async-start | bytes 1048576 | tf_op jit(solution)/shard_map/all_to_all | solution.py:37
  269.1 1.1 select_reduce_fusion
  272.1 1.4 reshape.70
  273.5 2.1 copy.49
  275.7 3.9 %reshape.68 = bf16[4096,1,32]{2,1,0:T(2,128)(2,1)S(1)} reshape(bf16[32,2,2048]{2,1,0:T(2,128)(2,1)} %all-to-all-done.2) | data formatting | bytes 524288
  279.6 3.5 %copy.43 = bf16[1,32,4096]{2,1,0:T(8,128)(2,1)} copy(bf16[1,32,4096]{1,0,2:T(2,128)(2,1)S(1)} %bitcast.82) | data formatting | bytes 524288 | tf_op jit(solution)/shard_map/all_to_all | solution.py:35
  283.1 1.0 copy.60
  285.0 3.9 %reshape.64 = bf16[4096,1,32]{2,1,0:T(2,128)(2,1)S(1)} reshape(bf16[32,2,2048]{2,1,0:T(2,128)(2,1)} %copy-done) | data formatting | bytes 524288
  288.8 3.5 %copy.37 = bf16[1,32,4096]{2,1,0:T(8,128)(2,1)} copy(bf16[1,32,4096]{1,0,2:T(2,128)(2,1)S(1)} %bitcast.83) | data formatting | bytes 524288 | tf_op jit(solution)/shard_map/all_to_all | solution.py:36
  292.3 1.0 copy.59
  293.4 0.8 copy.38
  294.2 1.0 reshape.62
  295.2 2.5 copy.54
  297.7 1.0 reshape.66
  298.7 2.5 copy.56
  301.2 1.0 pad_maximum_fusion.1
  302.2 1.0 pad_maximum_fusion
  303.2 3.1 fusion
  306.4 3.2 fusion.1
  309.5 3.2 fusion.18
  313.2 2.2 reduce.9
  315.4 27.7 %all_to_all.105 = bf16[32,2,2048]{2,1,0:T(2,128)(2,1)S(1)} all-to-all(bf16[32,2,2048]{2,1,0:T(2,128)(2,1)S(1)} %reshape.71), channel_id=1, replica_groups=mesh['span'=16,'seq'=32] {'seq'}, dimensions={0} | all-to-all | bytes 524288 | tf_op jit(solution)/shard_map/all_to_all | solution.py:78
  (36 shorter events, 7.2 us)
Async XLA Ops:
  29.2 44.4 %all-to-all-start.4 = ((bf16[32,2,2048]{2,1,0:T(2,128)(2,1)}), bf16[32,2,2048]{2,1,0:T(2,128)(2,1)S(1)}, u32[]{:S(2)}, u32[]{:S(2)}) async-start(bf16[32,2,2048]{2,1,0:T(2,128)(2,1)} %reshape.69), calls=%async_computation.4 | async-start | bytes 524288 | tf_op jit(solution)/shard_map/all_to_all | solution.py:34
  71.8 193.9 %copy-start.1 = (s32[16,2]{0,1:T(2,128)S(1)}, s32[16,2]{0,1:T(2,128)}, u32[]{:S(2)}) copy-start(s32[16,2]{0,1:T(2,128)} %param.11) | copy-start | bytes 388
  71.8 195.8 %copy-start.2 = (s32[16]{0:T(128)S(1)}, s32[16]{0:T(128)}, u32[]{:S(2)}) copy-start(s32[16]{0:T(128)} %param.10) | copy-start | bytes 196
  71.8 195.8 %copy-start.3 = (s32[16]{0:T(128)S(1)}, s32[16]{0:T(128)}, u32[]{:S(2)}) copy-start(s32[16]{0:T(128)} %param.12) | copy-start | bytes 196
  73.5 41.3 %all-to-all-start.2 = ((bf16[32,2,2048]{2,1,0:T(2,128)(2,1)}), bf16[32,2,2048]{2,1,0:T(2,128)(2,1)}, u32[]{:S(2)}, u32[]{:S(2)}) async-start(bf16[32,2,2048]{2,1,0:T(2,128)(2,1)} %reshape.67), calls=%async_computation.2 | async-start | bytes 524288 | tf_op jit(solution)/shard_map/all_to_all | solution.py:35
  114.9 46.7 %all-to-all-start = ((bf16[32,2,2048]{2,1,0:T(2,128)(2,1)}), bf16[32,2,2048]{2,1,0:T(2,128)(2,1)S(1)}, u32[]{:S(2)}, u32[]{:S(2)}) async-start(bf16[32,2,2048]{2,1,0:T(2,128)(2,1)} %reshape.63), calls=%async_computation | async-start | bytes 524288 | tf_op jit(solution)/shard_map/all_to_all | solution.py:36
  127.1 18.5 %collective-permute-start.1 = (bf16[1,32,4096]{2,1,0:T(8,128)(2,1)}, bf16[1,32,4096]{2,1,0:T(8,128)(2,1)S(1)}, u32[]{:S(2)}, u32[]{:S(2)}) collective-permute-start(bf16[1,32,4096]{2,1,0:T(8,128)(2,1)} %param.9), channel_id=1, source_target_pairs={{0,64},{32,96},{64,128},{96,160},{128,192},{160,224},{192,256},{22... | collective-permute-start | bytes 786440 | tf_op jit(solution)/shard_map/ppermute | solution.py:13
  135.3 20.7 %collective-permute-start = (bf16[1,32,4096]{2,1,0:T(8,128)(2,1)}, bf16[1,32,4096]{2,1,0:T(8,128)(2,1)S(1)}, u32[]{:S(2)}, u32[]{:S(2)}) collective-permute-start(bf16[1,32,4096]{2,1,0:T(8,128)(2,1)} %param.9), channel_id=1, source_target_pairs={{0,32},{32,64},{64,96},{96,128},{128,160},{160,192},{192,224},{224... | collective-permute-start | bytes 786440 | tf_op jit(solution)/shard_map/ppermute | solution.py:13
  161.5 50.7 %copy-start = (bf16[32,2,2048]{2,1,0:T(2,128)(2,1)}, bf16[32,2,2048]{2,1,0:T(2,128)(2,1)S(1)}, u32[]{:S(2)}) copy-start(bf16[32,2,2048]{2,1,0:T(2,128)(2,1)S(1)} %all-to-all-done) | copy-start | bytes 786436
  161.5 67.4 %all-to-all-start.1 = ((bf16[32,2,4096]{2,1,0:T(2,128)(2,1)}), bf16[32,2,4096]{2,1,0:T(2,128)(2,1)S(1)}, u32[]{:S(2)}, u32[]{:S(2)}) async-start(bf16[32,2,4096]{2,1,0:T(2,128)(2,1)} %reshape.61), calls=%async_computation.1 | async-start | bytes 1048576 | tf_op jit(solution)/shard_map/all_to_all | solution.py:38
  193.2 19.0 %collective-permute-start.3 = (bf16[1,32,4096]{2,1,0:T(8,128)(2,1)}, bf16[1,32,4096]{2,1,0:T(8,128)(2,1)S(1)}, u32[]{:S(2)}, u32[]{:S(2)}) collective-permute-start(bf16[1,32,4096]{2,1,0:T(8,128)(2,1)} %param.8), channel_id=1, source_target_pairs={{0,64},{32,96},{64,128},{96,160},{128,192},{160,224},{192,256},{22... | collective-permute-start | bytes 786440 | tf_op jit(solution)/shard_map/ppermute | solution.py:13
  198.6 18.5 %collective-permute-start.2 = (bf16[1,32,4096]{2,1,0:T(8,128)(2,1)}, bf16[1,32,4096]{2,1,0:T(8,128)(2,1)S(1)}, u32[]{:S(2)}, u32[]{:S(2)}) collective-permute-start(bf16[1,32,4096]{2,1,0:T(8,128)(2,1)} %param.8), channel_id=1, source_target_pairs={{0,32},{32,64},{64,96},{96,128},{128,160},{160,192},{192,224},{224... | collective-permute-start | bytes 786440 | tf_op jit(solution)/shard_map/ppermute | solution.py:13
  229.0 68.7 %all-to-all-start.3 = ((bf16[32,2,4096]{2,1,0:T(2,128)(2,1)}), bf16[32,2,4096]{2,1,0:T(2,128)(2,1)S(1)}, u32[]{:S(2)}, u32[]{:S(2)}) async-start(bf16[32,2,4096]{2,1,0:T(2,128)(2,1)} %reshape.65), calls=%async_computation.3 | async-start | bytes 1048576 | tf_op jit(solution)/shard_map/all_to_all | solution.py:37
where the time goes:
time: 347 us; the launch traced here: 344 us
  starting transfers between devices  126 us (36%)
  other arithmetic  79.1 us (23%)
  local copies, waits for them, and re-layouts  61.3 us (18%)
  waiting for transfers between devices  41.7 us (12%)
  blocking collectives  27.7 us (8%)
  matrix products  6.32 us (2%)
    unnamed x4, other arithmetic  69.4 us
    unnamed x28, local copies, waits for them, and re-layouts  38.2 us
    all_to_all x1, starting transfers between devices, per_device(): lax.all_to_all(earlier_keys, 'seq', split_axis=2, concat_axis=1, tiled=True)  36.7 us
    ppermute x4, waiting for transfers between devices, shifted(): lax.ppermute(value, axis, [(source, source + steps) for source in range(l...  35.3 us
    all_to_all x1, starting transfers between devices, per_device(): lax.all_to_all(earlier_values, 'seq', split_axis=2, concat_axis=1, tiled=...  31.7 us
    all_to_all x1, blocking collectives, per_device(): return lax.all_to_all(gated, 'seq', split_axis=1, concat_axis=2, tiled=True)  27.7 us
    ppermute x4, starting transfers between devices, shifted(): lax.ppermute(value, axis, [(source, source + steps) for source in range(l...  17.4 us
    all_to_all x1, starting transfers between devices, per_device(): lax.all_to_all(queries, 'seq', split_axis=2, concat_axis=1, tiled=True)  15.7 us
  transfers between devices with their start and end apart: 9, of which 5 were waited for; matrix products, arithmetic and copies ran while one was open for 29% of the time, Pallas kernels for 0%

commit v1 on v0

v1 whole, which is shorter than its diff:
```python
import functools

import jax
import jax.numpy as jnp
from jax import lax
from jax.experimental import pallas as pl
from jax.experimental.pallas import tpu as pltpu
from jax.sharding import PartitionSpec as P

HD = 128
WIN = 2
NX, NY, NZ = 4, 4, 8
CORES = 2
QB = 128
MESH = pl.DeviceIdType.MESH
NEG = -1e30
LOG2E = 1.4426950408889634


def low_bit(pair):
    return 1 - lax.rem(pair + 2, 8) // 4


def attend_kernel(
    lengths, span_mask, levels, q_in, k_in, v_in, gain_in, out,
    q_buf, k_buf, v_buf, o_buf, gain_buf,
    send_k, send_v, send_q, send_o, send_shift,
    recv_k, recv_v, recv_q, recv_o, gain_sem,
):
    rows = q_in.shape[0]
    slots = k_buf.shape[1]
    span_count = lengths.shape[0]
    chunk = slots // NY
    here = lax.axis_index("span")
    member = lax.axis_index("seq")
    x, z_hi, core = here // 4, lax.rem(here // 2, 2), lax.rem(here, 2)
    y, z_lo = member // NZ, lax.rem(member, NZ)
    z = z_hi * NZ + z_lo
    pair, bit = z // 2, lax.rem(z, 2)
    upper = (bit + low_bit(pair)) - 2 * bit * low_bit(pair)
    span = 4 * x + 2 * upper + core
    head = y * NZ + pair
    stays = upper == z_hi

    def device(xx, yy, zz, cc):
        return (xx * 4 + (zz // NZ) * 2 + cc, yy * NZ + lax.rem(zz, NZ))

    def head_place(pp):
        first = low_bit(pp)
        return 2 * pp + first + z_hi * (1 - 2 * first)

    flipped = z + 1 - 2 * bit
    next_x = lax.rem(x + upper, NX)
    prev_x = lax.rem(x + NX - 1 + upper, NX)

    barrier = pltpu.get_barrier_semaphore()

    def greet(index, carry):
        yy, zz = index // NZ, lax.rem(index, NZ)

        @pl.when(jnp.logical_not(stays & (index == member)))
        def _():
            pl.semaphore_signal(
                barrier, inc=1, device_id=device(x, yy, upper * NZ + zz, core), device_id_type=MESH
            )

        return carry

    lax.fori_loop(0, NY * NZ, greet, 0)

    @pl.when(core == 0)
    def _():
        for cc in range(CORES):
            pl.semaphore_signal(
                barrier, inc=1, device_id=device(prev_x, y, flipped, cc), device_id_type=MESH
            )

    @pl.when(core == 1)
    def _():
        pl.semaphore_signal(barrier, inc=1, device_id=device(x, y, z, 0), device_id_type=MESH)

    gain_copy = pltpu.make_async_copy(
        gain_in.at[:, pl.ds(pl.multiple_of(head * HD, HD), HD)], gain_buf, gain_sem
    )
    gain_copy.start()

    pl.semaphore_wait(barrier, NY * NZ + 2 - core - jnp.where(stays, 1, 0))

    def exchange(source, landing, send_sem, recv_sem):
        def step(index, carry):
            turn, place = index // NZ, NZ - 1 - lax.rem(index, NZ)
            yy = lax.rem(y + turn, NY)
            away = ((place + 1) // 2) * (2 * lax.rem(place, 2) - 1)
            pp = lax.rem(pair + away + NZ, NZ)
            zz = head_place(pp)
            columns = pl.ds(pl.multiple_of((yy * NZ + pp) * HD, HD), HD)
            block = source.at[:, columns]
            target = landing.at[pl.ds(pl.multiple_of(member * rows, rows), rows), :]
            own = (yy == y) & (zz == z)

            @pl.when(own)
            def _():
                pltpu.make_async_copy(block, target, recv_sem).start()

            @pl.when(jnp.logical_not(own))
            def _():
                pltpu.make_async_remote_copy(
                    src_ref=block, dst_ref=target, send_sem=send_sem, recv_sem=recv_sem,
                    device_id=device(x, yy, zz, core), device_id_type=MESH,
                ).start()

            return carry

        lax.fori_loop(0, NY * NZ, step, 0)

    exchange(k_in, k_buf.at[0], send_k, recv_k.at[0])
    exchange(v_in, v_buf.at[0], send_v, recv_v.at[0])
    exchange(q_in, q_buf, send_q, recv_q.at[y])

    def landed(ref, sem):
        pltpu.make_async_copy(ref, ref, sem).wait()

    def shift(buf, from_slot, to_slot, send_sem, recv, target):
        return pltpu.make_async_remote_copy(
            src_ref=buf.at[from_slot], dst_ref=buf.at[to_slot], send_sem=send_sem,
            recv_sem=recv.at[to_slot], device_id=target, device_id_type=MESH,
        )

    for which, (buf, recv) in enumerate(((k_buf, recv_k), (v_buf, recv_v))):
        landed(buf.at[0], recv.at[0])

        @pl.when(core == 0)
        def _():
            shift(buf, 0, 2, send_shift.at[3 * which], recv, device(next_x, y, flipped, 0)).start()
            shift(buf, 0, 1, send_shift.at[3 * which + 1], recv, device(x, y, z, 1)).start()

        @pl.when(core == 1)
        def _():
            shift(buf, 0, 1, send_shift.at[3 * which], recv, device(next_x, y, flipped, 0)).start()

    for which, (buf, recv) in enumerate(((k_buf, recv_k), (v_buf, recv_v))):
        landed(buf.at[1], recv.at[1])

        @pl.when(core == 0)
        def _():
            shift(buf, 1, 2, send_shift.at[3 * which + 2], recv, device(x, y, z, 1)).start()

    limits = []
    for step in range(WIN + 1):
        earlier = jnp.maximum(span - step, 0)
        limit = lengths[earlier]
        if step > 0:
            limit = jnp.where((span - step >= 0) & (span_mask[span, step - 1] == 1), limit, 0)
        limits.append(limit)
    gain_copy.wait()
    level = levels[span]
    gain_row = jnp.sum(
        jnp.where(lax.broadcasted_iota(jnp.int32, gain_buf.shape, 0) == level, gain_buf[...], 0.0),
        axis=0, keepdims=True,
    )
    scale = LOG2E / (HD ** 0.5)

    for buf, recv in ((k_buf, recv_k), (v_buf, recv_v)):
        landed(buf.at[2], recv.at[2])

    def attend(turn, carry):
        yy = lax.rem(y + NY - turn, NY)
        base = pl.multiple_of(yy * chunk, chunk)
        landed(q_buf.at[pl.ds(base, chunk), :], recv_q.at[yy])

        def block(index, inner):
            spot = pl.ds(pl.multiple_of(base + index * QB, QB), QB)
            queries = q_buf[spot, :]
            scores = []
            for step in range(WIN + 1):
                part = lax.dot_general(
                    queries, k_buf[step], (((1,), (1,)), ((), ())), preferred_element_type=jnp.float32
                )
                live = lax.broadcasted_iota(jnp.int32, (1, slots), 1) < limits[step]
                scores.append(jnp.where(live, part, NEG))
            top = functools.reduce(
                jnp.maximum, [jnp.max(part, axis=-1, keepdims=True) for part in scores]
            )
            total = jnp.zeros((QB, 1), jnp.float32)
            mixed = jnp.zeros((QB, HD), jnp.float32)
            for step in range(WIN + 1):
                expd = jnp.exp2((scores[step] - top) * scale)
                total += jnp.sum(expd, axis=-1, keepdims=True)
                mixed += jnp.dot(
                    expd.astype(jnp.bfloat16), v_buf[step], preferred_element_type=jnp.float32
                )
            o_buf[spot, :] = (mixed / total * gain_row).astype(jnp.bfloat16)
            return inner

        lax.fori_loop(0, chunk // QB, block, 0)

        def give(zz, inner):
            block_rows = pl.ds(pl.multiple_of(base + zz * rows, rows), rows)
            done = o_buf.at[block_rows, :]
            target = out.at[:, pl.ds(pl.multiple_of(head * HD, HD), HD)]
            own = stays & (yy == y) & (zz == z_lo)

            @pl.when(own)
            def _():
                pltpu.make_async_copy(done, target, recv_o).start()

            @pl.when(jnp.logical_not(own))
            def _():
                pltpu.make_async_remote_copy(
                    src_ref=done, dst_ref=target, send_sem=send_o, recv_sem=recv_o,
                    device_id=device(x, yy, upper * NZ + zz, core), device_id_type=MESH,
                ).start()

            return inner

        lax.fori_loop(0, NZ, give, 0)
        return carry

    lax.fori_loop(0, NY, attend, 0)

    landed(out, recv_o)
    remote = (NY * NZ - 1) * HD
    for ref, sem in ((k_in, send_k), (v_in, send_v), (q_in, send_q), (q_in, send_o)):
        landed(ref.at[:, pl.ds(0, remote)], sem)

        @pl.when(jnp.logical_not(stays))
        def _():
            landed(ref.at[:, pl.ds(remote, HD)], sem)

    for which, buf in enumerate((k_buf, v_buf)):
        landed(buf.at[0], send_shift.at[3 * which])

        @pl.when(core == 0)
        def _():
            landed(buf.at[0], send_shift.at[3 * which + 1])
            landed(buf.at[1], send_shift.at[3 * which + 2])


def per_device(queries, keys, values, lengths, span_mask, levels, level_gain):
    _, rows, width = queries.shape
    slots = rows * NY * NZ
    hbm = pl.BlockSpec(memory_space=pl.ANY)
    smem = pl.BlockSpec(memory_space=pltpu.SMEM)
    dma = pltpu.SemaphoreType.DMA
    result = pl.pallas_call(
        attend_kernel,
        out_shape=jax.ShapeDtypeStruct((rows, width), jnp.bfloat16),
        in_specs=[smem, smem, smem, hbm, hbm, hbm, hbm],
        out_specs=hbm,
        scratch_shapes=[
            pltpu.VMEM((slots, HD), jnp.bfloat16),
            pltpu.VMEM((WIN + 1, slots, HD), jnp.bfloat16),
            pltpu.VMEM((WIN + 1, slots, HD), jnp.bfloat16),
            pltpu.VMEM((slots, HD), jnp.bfloat16),
            pltpu.VMEM((level_gain.shape[0], HD), jnp.float32),
            dma, dma, dma, dma, dma((6,)),
            dma((WIN + 1,)), dma((WIN + 1,)), dma((NY,)), dma, dma,
        ],
        compiler_params=pltpu.CompilerParams(
            collective_id=0, has_side_effects=True, vmem_limit_bytes=32 * 1024 * 1024
        ),
    )(lengths, span_mask, levels, queries[0], keys[0], values[0], level_gain)
    return result[None]


def solution(mesh):
    placed = (
        P("span", "seq", None),
        P("span", "seq", None),
        P("span", "seq", None),
        P(),
        P(),
        P(),
        P(),
    )
    return jax.shard_map(
        per_device, mesh=mesh, in_specs=placed, out_specs=P("span", "seq", None), check_vma=False
    )
```

time: 347 us -> 87.2 us (0.25)
  the two profiles are of different devices: /device:TPU:6 before, /device:TPU:1 now
where the time goes in v1:
time: 87.2 us; the launch traced here: 86.9 us
  Pallas kernels  81.1 us (93%)
  local copies, waits for them, and re-layouts  5.85 us (7%)
    pallas_call x1, Pallas kernels, per_device(): pl.pallas_call(attend_kernel, out_shape=jax.ShapeDtypeStruct((rows, width...  81.1 us
    unnamed x16, local copies, waits for them, and re-layouts  5.85 us

profile of v1, /device:TPU:1, one launch (start us, length us, event | category | flops | bytes accessed | tf_op | source)
XLA Modules:
  0.0 86.9 jit_solution(17062221234592520868)
XLA Ops:
  0.0 0.0 copy-start.6
  0.0 0.7 copy-done.6
  0.7 0.0 copy-start.4
  0.7 0.0 copy-start.5
  0.7 0.1 copy.8.span_mask
  0.8 0.6 copy-done.4
  1.3 0.0 copy-done.5
  1.4 0.0 copy-start
  1.4 0.9 %copy-done = bf16[1,32,4096]{2,1,0:T(8,128)(2,1)S(1)} copy-done((bf16[1,32,4096]{2,1,0:T(8,128)(2,1)S(1)}, bf16[1,32,4096]{2,1,0:T(8,128)(2,1)}, u32[]{:S(2)}) %copy-start) | copy-done | bytes 262168
  2.3 0.0 copy-start.1
  2.3 0.9 %copy-done.1 = bf16[1,32,4096]{2,1,0:T(8,128)(2,1)S(1)} copy-done((bf16[1,32,4096]{2,1,0:T(8,128)(2,1)S(1)}, bf16[1,32,4096]{2,1,0:T(8,128)(2,1)}, u32[]{:S(2)}) %copy-start.1) | copy-done | bytes 262168
  3.3 0.0 copy-start.2
  3.3 0.9 %copy-done.2 = bf16[1,32,4096]{2,1,0:T(8,128)(2,1)S(1)} copy-done((bf16[1,32,4096]{2,1,0:T(8,128)(2,1)S(1)}, bf16[1,32,4096]{2,1,0:T(8,128)(2,1)}, u32[]{:S(2)}) %copy-start.2) | copy-done | bytes 262168
  4.2 0.0 copy-start.3
  4.2 0.9 %copy-done.3 = f32[16,4096]{1,0:T(8,128)S(1)} copy-done((f32[16,4096]{1,0:T(8,128)S(1)}, f32[16,4096]{1,0:T(8,128)}, u32[]{:S(2)}) %copy-start.3) | copy-done | bytes 262168
  5.2 81.1 %shard_map.73 = bf16[32,4096]{1,0:T(8,128)(2,1)S(1)} custom-call(s32[16]{0:T(128)S(1)} %copy-done.4, s32[16,2]{1,0:T(8,128)S(1)} %copy.8.span_mask, s32[16]{0:T(128)S(1)} %copy-done.5, bf16[32,4096]{1,0:T(8,128)(2,1)S(1)} %bitcast.5, bf16[32,4096]{1,0:T(8,128)(2,1)S(1)} %bitcast.6, bf16[32,4096]{1,0:T(8,128)(2,1)S(1)} %bitcast.7, f32[16,4096]{1,0:T(8,128)S(1)} %copy-done.3), custom_call_target="tpu_custom_call" | custom-call | tf_op jit(solution)/shard_map/pallas_call | solution.py:245
  86.2 0.7 copy.10
Async XLA Ops:
  0.0 0.7 copy-start.6
  0.7 0.7 copy-start.4
  0.7 0.7 copy-start.5
  1.4 0.9 %copy-start = (bf16[1,32,4096]{2,1,0:T(8,128)(2,1)S(1)}, bf16[1,32,4096]{2,1,0:T(8,128)(2,1)}, u32[]{:S(2)}) copy-start(bf16[1,32,4096]{2,1,0:T(8,128)(2,1)} %param.7) | copy-start | bytes 786436
  2.3 0.9 %copy-start.1 = (bf16[1,32,4096]{2,1,0:T(8,128)(2,1)S(1)}, bf16[1,32,4096]{2,1,0:T(8,128)(2,1)}, u32[]{:S(2)}) copy-start(bf16[1,32,4096]{2,1,0:T(8,128)(2,1)} %param.8) | copy-start | bytes 786436
  3.3 0.9 %copy-start.2 = (bf16[1,32,4096]{2,1,0:T(8,128)(2,1)S(1)}, bf16[1,32,4096]{2,1,0:T(8,128)(2,1)}, u32[]{:S(2)}) copy-start(bf16[1,32,4096]{2,1,0:T(8,128)(2,1)} %param.9) | copy-start | bytes 786436
  4.2 0.9 %copy-start.3 = (f32[16,4096]{1,0:T(8,128)S(1)}, f32[16,4096]{1,0:T(8,128)}, u32[]{:S(2)}) copy-start(f32[16,4096]{1,0:T(8,128)} %gain_in.1) | copy-start | bytes 786436

commit v2 on v1

--- a/solution.py
+++ b/solution.py
@@ -17,8 +17,8 @@
 LOG2E = 1.4426950408889634
 
 
-def low_bit(pair):
-    return 1 - lax.rem(pair + 2, 8) // 4
+def group_x(group):
+    return jnp.where(group < 4, lax.rem(group + 3, NX), lax.rem(10 - group, NX))
 
 
 def attend_kernel(
@@ -36,22 +36,28 @@
     x, z_hi, core = here // 4, lax.rem(here // 2, 2), lax.rem(here, 2)
     y, z_lo = member // NZ, lax.rem(member, NZ)
     z = z_hi * NZ + z_lo
-    pair, bit = z // 2, lax.rem(z, 2)
-    upper = (bit + low_bit(pair)) - 2 * bit * low_bit(pair)
-    span = 4 * x + 2 * upper + core
-    head = y * NZ + pair
-    stays = upper == z_hi
+    home = 2 * x + z_hi
+    odd = lax.rem(y + z, 2)
+    group = jnp.where(odd == 0, lax.rem(x + 1, NX), NX + lax.rem(6 - x, NX))
+    span = CORES * group + core
+    head = (y // 2) * (2 * NZ) + z
+    stays = group == home
+    first, last = group == 0, group == 2 * NX - 1
 
     def device(xx, yy, zz, cc):
         return (xx * 4 + (zz // NZ) * 2 + cc, yy * NZ + lax.rem(zz, NZ))
 
-    def head_place(pp):
-        first = low_bit(pp)
-        return 2 * pp + first + z_hi * (1 - 2 * first)
-
-    flipped = z + 1 - 2 * bit
-    next_x = lax.rem(x + upper, NX)
-    prev_x = lax.rem(x + NX - 1 + upper, NX)
+    def token_place(yy, zz):
+        return device(group // 2, yy, lax.rem(group, 2) * NZ + zz, core)
+
+    def beside(other, cc):
+        return device(group_x(other), 2 * (y // 2) + lax.rem(other // NX + z, 2), z, cc)
+
+    def after(cc):
+        return beside(lax.rem(group + 1, 2 * NX), cc)
+
+    def before(cc):
+        return beside(lax.rem(group + 2 * NX - 1, 2 * NX), cc)
 
     barrier = pltpu.get_barrier_semaphore()
 
@@ -61,42 +67,42 @@
         @pl.when(jnp.logical_not(stays & (index == member)))
         def _():
             pl.semaphore_signal(
-                barrier, inc=1, device_id=device(x, yy, upper * NZ + zz, core), device_id_type=MESH
+                barrier, inc=1, device_id=token_place(yy, zz), device_id_type=MESH
             )
 
         return carry
 
     lax.fori_loop(0, NY * NZ, greet, 0)
 
-    @pl.when(core == 0)
+    @pl.when((core == 0) & jnp.logical_not(first))
     def _():
         for cc in range(CORES):
-            pl.semaphore_signal(
-                barrier, inc=1, device_id=device(prev_x, y, flipped, cc), device_id_type=MESH
-            )
+            pl.semaphore_signal(barrier, inc=1, device_id=before(cc), device_id_type=MESH)
 
     @pl.when(core == 1)
     def _():
-        pl.semaphore_signal(barrier, inc=1, device_id=device(x, y, z, 0), device_id_type=MESH)
+        pl.semaphore_signal(barrier, inc=1, device_id=beside(group, 0), device_id_type=MESH)
 
     gain_copy = pltpu.make_async_copy(
         gain_in.at[:, pl.ds(pl.multiple_of(head * HD, HD), HD)], gain_buf, gain_sem
     )
     gain_copy.start()
 
-    pl.semaphore_wait(barrier, NY * NZ + 2 - core - jnp.where(stays, 1, 0))
+    pl.semaphore_wait(
+        barrier, NY * NZ + 2 - core - jnp.where(stays, 1, 0) - jnp.where(last, 1, 0)
+    )
 
     def exchange(source, landing, send_sem, recv_sem):
         def step(index, carry):
-            turn, place = index // NZ, NZ - 1 - lax.rem(index, NZ)
-            yy = lax.rem(y + turn, NY)
+            turn, place = index // (2 * NZ), 2 * NZ - 1 - lax.rem(index, 2 * NZ)
+            half = lax.rem(y // 2 + turn, 2)
             away = ((place + 1) // 2) * (2 * lax.rem(place, 2) - 1)
-            pp = lax.rem(pair + away + NZ, NZ)
-            zz = head_place(pp)
-            columns = pl.ds(pl.multiple_of((yy * NZ + pp) * HD, HD), HD)
+            zz = lax.rem(z + away + 2 * NZ, 2 * NZ)
+            yy = 2 * half + lax.rem(home // NX + zz, 2)
+            columns = pl.ds(pl.multiple_of((half * 2 * NZ + zz) * HD, HD), HD)
             block = source.at[:, columns]
             target = landing.at[pl.ds(pl.multiple_of(member * rows, rows), rows), :]
-            own = (yy == y) & (zz == z)
+            own = stays & (yy == y) & (zz == z)
 
             @pl.when(own)
             def _():
@@ -106,7 +112,7 @@
             def _():
                 pltpu.make_async_remote_copy(
                     src_ref=block, dst_ref=target, send_sem=send_sem, recv_sem=recv_sem,
-                    device_id=device(x, yy, zz, core), device_id_type=MESH,
+                    device_id=device(group_x(home), yy, zz, core), device_id_type=MESH,
                 ).start()
 
             return carry
@@ -126,24 +132,43 @@
             recv_sem=recv.at[to_slot], device_id=target, device_id_type=MESH,
         )
 
+    @pl.when(first)
+    def _():
+        @pl.when(core == 0)
+        def _():
+            k_buf[1] = jnp.zeros(k_buf.shape[1:], k_buf.dtype)
+            v_buf[1] = jnp.zeros(v_buf.shape[1:], v_buf.dtype)
+
+        k_buf[2] = jnp.zeros(k_buf.shape[1:], k_buf.dtype)
+        v_buf[2] = jnp.zeros(v_buf.shape[1:], v_buf.dtype)
+
+    ahead = jnp.logical_not(last)
     for which, (buf, recv) in enumerate(((k_buf, recv_k), (v_buf, recv_v))):
         landed(buf.at[0], recv.at[0])
 
         @pl.when(core == 0)
         def _():
-            shift(buf, 0, 2, send_shift.at[3 * which], recv, device(next_x, y, flipped, 0)).start()
-            shift(buf, 0, 1, send_shift.at[3 * which + 1], recv, device(x, y, z, 1)).start()
+            @pl.when(ahead)
+            def _():
+                shift(buf, 0, 2, send_shift.at[3 * which], recv, after(0)).start()
+
+            shift(buf, 0, 1, send_shift.at[3 * which + 1], recv, beside(group, 1)).start()
+
+        @pl.when((core == 1) & ahead)
+        def _():
+            shift(buf, 0, 1, send_shift.at[3 * which], recv, after(0)).start()
+
+    behind = jnp.logical_not(first)
+    for which, (buf, recv) in enumerate(((k_buf, recv_k), (v_buf, recv_v))):
+
+        @pl.when((core == 0) & behind)
+        def _():
+            landed(buf.at[1], recv.at[1])
+            shift(buf, 1, 2, send_shift.at[3 * which + 2], recv, beside(group, 1)).start()
 
         @pl.when(core == 1)
         def _():
-            shift(buf, 0, 1, send_shift.at[3 * which], recv, device(next_x, y, flipped, 0)).start()
-
-    for which, (buf, recv) in enumerate(((k_buf, recv_k), (v_buf, recv_v))):
-        landed(buf.at[1], recv.at[1])
-
-        @pl.when(core == 0)
-        def _():
-            shift(buf, 1, 2, send_shift.at[3 * which + 2], recv, device(x, y, z, 1)).start()
+            landed(buf.at[1], recv.at[1])
 
     limits = []
     for step in range(WIN + 1):
@@ -160,11 +185,15 @@
     )
     scale = LOG2E / (HD ** 0.5)
 
-    for buf, recv in ((k_buf, recv_k), (v_buf, recv_v)):
-        landed(buf.at[2], recv.at[2])
+    @pl.when(behind)
+    def _():
+        for buf, recv in ((k_buf, recv_k), (v_buf, recv_v)):
+            landed(buf.at[2], recv.at[2])
+
+    near_run = jnp.where(lax.rem(group, 2) == z_hi, NZ // 2, 0)
 
     def attend(turn, carry):
-        yy = lax.rem(y + NY - turn, NY)
+        yy = lax.rem(y - lax.rem(y, 2) + turn, NY)
         base = pl.multiple_of(yy * chunk, chunk)
         landed(q_buf.at[pl.ds(base, chunk), :], recv_q.at[yy])
 
@@ -194,7 +223,9 @@
 
         lax.fori_loop(0, chunk // QB, block, 0)
 
-        def give(zz, inner):
+        def give(index, inner):
+            away = ((index + 1) // 2) * (2 * lax.rem(index, 2) - 1)
+            zz = lax.rem(z_lo + near_run + away + NZ, NZ)
             block_rows = pl.ds(pl.multiple_of(base + zz * rows, rows), rows)
             done = o_buf.at[block_rows, :]
             target = out.at[:, pl.ds(pl.multiple_of(head * HD, HD), HD)]
@@ -208,7 +239,7 @@
             def _():
                 pltpu.make_async_remote_copy(
                     src_ref=done, dst_ref=target, send_sem=send_o, recv_sem=recv_o,
-                    device_id=device(x, yy, upper * NZ + zz, core), device_id_type=MESH,
+                    device_id=token_place(yy, zz), device_id_type=MESH,
                 ).start()
 
             return inner
@@ -228,11 +259,17 @@
             landed(ref.at[:, pl.ds(remote, HD)], sem)
 
     for which, buf in enumerate((k_buf, v_buf)):
-        landed(buf.at[0], send_shift.at[3 * which])
+
+        @pl.when(ahead)
+        def _():
+            landed(buf.at[0], send_shift.at[3 * which])
 
         @pl.when(core == 0)
         def _():
             landed(buf.at[0], send_shift.at[3 * which + 1])
+
+        @pl.when((core == 0) & behind)
+        def _():
             landed(buf.at[1], send_shift.at[3 * which + 2])
 
 
@@ -246,7 +283,7 @@
         attend_kernel,
         out_shape=jax.ShapeDtypeStruct((rows, width), jnp.bfloat16),
         in_specs=[smem, smem, smem, hbm, hbm, hbm, hbm],
-        out_specs=hbm,
+        out_specs=pl.BlockSpec(memory_space=pl.ANY),
         scratch_shapes=[
             pltpu.VMEM((slots, HD), jnp.bfloat16),
             pltpu.VMEM((WIN + 1, slots, HD), jnp.bfloat16),
@@ -257,7 +294,7 @@
             dma((WIN + 1,)), dma((WIN + 1,)), dma((NY,)), dma, dma,
         ],
         compiler_params=pltpu.CompilerParams(
-            collective_id=0, has_side_effects=True, vmem_limit_bytes=32 * 1024 * 1024
+            collective_id=0, has_side_effects=True, vmem_limit_bytes=60 * 1024 * 1024
         ),
     )(lengths, span_mask, levels, queries[0], keys[0], values[0], level_gain)
     return result[None]

time: 87.2 us -> 76.5 us (0.88)
  the two profiles are of different devices: /device:TPU:1 before, /device:TPU:8 now
where the time goes in v2:
time: 76.5 us; the launch traced here: 76.3 us
  Pallas kernels  73.3 us (96%)
  local copies, waits for them, and re-layouts  3.03 us (4%)
    pallas_call x1, Pallas kernels, per_device(): pl.pallas_call(attend_kernel, out_shape=jax.ShapeDtypeStruct((rows, width...  73.3 us
    unnamed x4, local copies, waits for them, and re-layouts  3.03 us

profile of v2, /device:TPU:8, one launch (start us, length us, event | category | flops | bytes accessed | tf_op | source)
XLA Modules:
  0.0 76.3 jit_solution(9311036289482541622)
XLA Ops:
  0.0 0.0 copy-start
  0.0 0.7 copy-done
  0.7 0.7 copy.8.span_mask
  1.4 73.3 %shard_map.73 = bf16[32,4096]{1,0:T(8,128)(2,1)} custom-call(s32[16]{0:T(128)} %lengths.1, s32[16,2]{1,0:T(8,128)} %copy.8.span_mask, s32[16]{0:T(128)} %levels.1, bf16[32,4096]{1,0:T(8,128)(2,1)} %bitcast.5, bf16[32,4096]{1,0:T(8,128)(2,1)} %bitcast.6, bf16[32,4096]{1,0:T(8,128)(2,1)} %bitcast.7, f32[16,4096]{1,0:T(8,128)} %gain_in.1), custom_call_target="tpu_custom_call" | custom-call | tf_op jit(solution)/shard_map/pallas_call | solution.py:282
  74.6 1.7 %copy.10 = bf16[1,32,4096]{2,1,0:T(8,128)(2,1)} copy(bf16[1,32,4096]{2,1,0:T(8,128)(2,1)} %bitcast.4) | data formatting | bytes 524288
Async XLA Ops:
  0.0 0.7 copy-start

commit v3 on v2

--- a/solution.py
+++ b/solution.py
@@ -22,14 +22,14 @@
 
 
 def attend_kernel(
-    lengths, span_mask, levels, q_in, k_in, v_in, gain_in, out,
+    lengths_in, mask_in, levels_in, q_in, k_in, v_in, gain_in, out,
+    lengths, span_mask, levels,
     q_buf, k_buf, v_buf, o_buf, gain_buf,
     send_k, send_v, send_q, send_o, send_shift,
-    recv_k, recv_v, recv_q, recv_o, gain_sem,
+    recv_k, recv_v, recv_q, recv_o, gain_sem, scalar_sem,
 ):
     rows = q_in.shape[0]
     slots = k_buf.shape[1]
-    span_count = lengths.shape[0]
     chunk = slots // NY
     here = lax.axis_index("span")
     member = lax.axis_index("seq")
@@ -37,7 +37,7 @@
     y, z_lo = member // NZ, lax.rem(member, NZ)
     z = z_hi * NZ + z_lo
     home = 2 * x + z_hi
-    odd = lax.rem(y + z, 2)
+    odd = lax.rem(y + core, 2)
     group = jnp.where(odd == 0, lax.rem(x + 1, NX), NX + lax.rem(6 - x, NX))
     span = CORES * group + core
     head = (y // 2) * (2 * NZ) + z
@@ -51,7 +51,7 @@
         return device(group // 2, yy, lax.rem(group, 2) * NZ + zz, core)
 
     def beside(other, cc):
-        return device(group_x(other), 2 * (y // 2) + lax.rem(other // NX + z, 2), z, cc)
+        return device(group_x(other), 2 * (y // 2) + lax.rem(other // NX + cc, 2), z, cc)
 
     def after(cc):
         return beside(lax.rem(group + 1, 2 * NX), cc)
@@ -59,12 +59,27 @@
     def before(cc):
         return beside(lax.rem(group + 2 * NX - 1, 2 * NX), cc)
 
+    scalar_copies = [
+        pltpu.make_async_copy(source, held, scalar_sem.at[index])
+        for index, (source, held) in enumerate(
+            ((lengths_in, lengths), (mask_in, span_mask), (levels_in, levels))
+        )
+    ]
+    for copy in scalar_copies:
+        copy.start()
     barrier = pltpu.get_barrier_semaphore()
 
+    run = lax.rem(group, 2)
+    far = z_lo + jnp.where(run == z_hi, NZ // 2, 0) + NZ
+
+    def token_slot(index):
+        away = ((index + 1) // 2) * (2 * lax.rem(index, 2) - 1)
+        return lax.rem(far + away, NZ)
+
     def greet(index, carry):
-        yy, zz = index // NZ, lax.rem(index, NZ)
-
-        @pl.when(jnp.logical_not(stays & (index == member)))
+        yy, zz = lax.rem(index, NY), token_slot(index // NY)
+
+        @pl.when(jnp.logical_not(stays & (yy == y) & (zz == z_lo)))
         def _():
             pl.semaphore_signal(
                 barrier, inc=1, device_id=token_place(yy, zz), device_id_type=MESH
@@ -79,6 +94,10 @@
         for cc in range(CORES):
             pl.semaphore_signal(barrier, inc=1, device_id=before(cc), device_id_type=MESH)
 
+    @pl.when((core == 1) & jnp.logical_not(first))
+    def _():
+        pl.semaphore_signal(barrier, inc=1, device_id=before(1), device_id_type=MESH)
+
     @pl.when(core == 1)
     def _():
         pl.semaphore_signal(barrier, inc=1, device_id=beside(group, 0), device_id_type=MESH)
@@ -89,16 +108,16 @@
     gain_copy.start()
 
     pl.semaphore_wait(
-        barrier, NY * NZ + 2 - core - jnp.where(stays, 1, 0) - jnp.where(last, 1, 0)
-    )
-
-    def exchange(source, landing, send_sem, recv_sem):
+        barrier, NY * NZ + 2 - jnp.where(stays, 1, 0) - jnp.where(last, 1 + core, 0)
+    )
+
+    def exchange(source, landing, send_sem, recv_sem, turns=(0, 1)):
         def step(index, carry):
             turn, place = index // (2 * NZ), 2 * NZ - 1 - lax.rem(index, 2 * NZ)
             half = lax.rem(y // 2 + turn, 2)
             away = ((place + 1) // 2) * (2 * lax.rem(place, 2) - 1)
             zz = lax.rem(z + away + 2 * NZ, 2 * NZ)
-            yy = 2 * half + lax.rem(home // NX + zz, 2)
+            yy = 2 * half + lax.rem(home // NX + core, 2)
             columns = pl.ds(pl.multiple_of((half * 2 * NZ + zz) * HD, HD), HD)
             block = source.at[:, columns]
             target = landing.at[pl.ds(pl.multiple_of(member * rows, rows), rows), :]
@@ -117,11 +136,11 @@
 
             return carry
 
-        lax.fori_loop(0, NY * NZ, step, 0)
+        lax.fori_loop(2 * NZ * turns[0], 2 * NZ * (turns[-1] + 1), step, 0)
 
     exchange(k_in, k_buf.at[0], send_k, recv_k.at[0])
     exchange(v_in, v_buf.at[0], send_v, recv_v.at[0])
-    exchange(q_in, q_buf, send_q, recv_q.at[y])
+    exchange(q_in, q_buf, send_q, recv_q.at[y], (0,))
 
     def landed(ref, sem):
         pltpu.make_async_copy(ref, ref, sem).wait()
@@ -157,25 +176,18 @@
         @pl.when((core == 1) & ahead)
         def _():
             shift(buf, 0, 1, send_shift.at[3 * which], recv, after(0)).start()
-
+            shift(buf, 0, 2, send_shift.at[3 * which + 2], recv, after(1)).start()
+
+    exchange(q_in, q_buf, send_q, recv_q.at[y], (1,))
     behind = jnp.logical_not(first)
-    for which, (buf, recv) in enumerate(((k_buf, recv_k), (v_buf, recv_v))):
-
-        @pl.when((core == 0) & behind)
-        def _():
-            landed(buf.at[1], recv.at[1])
-            shift(buf, 1, 2, send_shift.at[3 * which + 2], recv, beside(group, 1)).start()
-
-        @pl.when(core == 1)
-        def _():
-            landed(buf.at[1], recv.at[1])
-
+    for copy in scalar_copies:
+        copy.wait()
     limits = []
     for step in range(WIN + 1):
         earlier = jnp.maximum(span - step, 0)
         limit = lengths[earlier]
         if step > 0:
-            limit = jnp.where((span - step >= 0) & (span_mask[span, step - 1] == 1), limit, 0)
+            limit = jnp.where((span - step >= 0) & (span_mask[step - 1, span] == 1), limit, 0)
         limits.append(limit)
     gain_copy.wait()
     level = levels[span]
@@ -185,47 +197,53 @@
     )
     scale = LOG2E / (HD ** 0.5)
 
-    @pl.when(behind)
-    def _():
-        for buf, recv in ((k_buf, recv_k), (v_buf, recv_v)):
+    for buf, recv in ((k_buf, recv_k), (v_buf, recv_v)):
+
+        @pl.when(behind)
+        def _():
             landed(buf.at[2], recv.at[2])
 
-    near_run = jnp.where(lax.rem(group, 2) == z_hi, NZ // 2, 0)
-
-    def attend(turn, carry):
+        @pl.when(behind | (core == 1))
+        def _():
+            landed(buf.at[1], recv.at[1])
+
+    per_chunk = chunk // QB
+    per_block = QB // rows
+
+    def attend(index, carry):
+        turn, part = index // per_chunk, lax.rem(index, per_chunk)
         yy = lax.rem(y - lax.rem(y, 2) + turn, NY)
         base = pl.multiple_of(yy * chunk, chunk)
-        landed(q_buf.at[pl.ds(base, chunk), :], recv_q.at[yy])
-
-        def block(index, inner):
-            spot = pl.ds(pl.multiple_of(base + index * QB, QB), QB)
-            queries = q_buf[spot, :]
-            scores = []
-            for step in range(WIN + 1):
-                part = lax.dot_general(
-                    queries, k_buf[step], (((1,), (1,)), ((), ())), preferred_element_type=jnp.float32
-                )
-                live = lax.broadcasted_iota(jnp.int32, (1, slots), 1) < limits[step]
-                scores.append(jnp.where(live, part, NEG))
-            top = functools.reduce(
-                jnp.maximum, [jnp.max(part, axis=-1, keepdims=True) for part in scores]
+
+        @pl.when(part == 0)
+        def _():
+            landed(q_buf.at[pl.ds(base, chunk), :], recv_q.at[yy])
+
+        first_slot = lax.rem(part + far // per_block, per_chunk) * per_block
+        spot = pl.ds(pl.multiple_of(base + first_slot * rows, QB), QB)
+        queries = q_buf[spot, :]
+        scores = []
+        for step in range(WIN + 1):
+            part_scores = lax.dot_general(
+                queries, k_buf[step], (((1,), (1,)), ((), ())), preferred_element_type=jnp.float32
             )
-            total = jnp.zeros((QB, 1), jnp.float32)
-            mixed = jnp.zeros((QB, HD), jnp.float32)
-            for step in range(WIN + 1):
-                expd = jnp.exp2((scores[step] - top) * scale)
-                total += jnp.sum(expd, axis=-1, keepdims=True)
-                mixed += jnp.dot(
-                    expd.astype(jnp.bfloat16), v_buf[step], preferred_element_type=jnp.float32
-                )
-            o_buf[spot, :] = (mixed / total * gain_row).astype(jnp.bfloat16)
-            return inner
-
-        lax.fori_loop(0, chunk // QB, block, 0)
-
-        def give(index, inner):
-            away = ((index + 1) // 2) * (2 * lax.rem(index, 2) - 1)
-            zz = lax.rem(z_lo + near_run + away + NZ, NZ)
+            live = lax.broadcasted_iota(jnp.int32, (1, slots), 1) < limits[step]
+            scores.append(jnp.where(live, part_scores, NEG))
+        top = functools.reduce(
+            jnp.maximum, [jnp.max(part_scores, axis=-1, keepdims=True) for part_scores in scores]
+        )
+        total = jnp.zeros((QB, 1), jnp.float32)
+        mixed = jnp.zeros((QB, HD), jnp.float32)
+        for step in range(WIN + 1):
+            expd = jnp.exp2((scores[step] - top) * scale)
+            total += jnp.sum(expd, axis=-1, keepdims=True)
+            mixed += jnp.dot(
+                expd.astype(jnp.bfloat16), v_buf[step], preferred_element_type=jnp.float32
+            )
+        o_buf[spot, :] = (mixed / total * gain_row).astype(jnp.bfloat16)
+
+        def give(offset, inner):
+            zz = first_slot + lax.rem(far + offset, per_block)
             block_rows = pl.ds(pl.multiple_of(base + zz * rows, rows), rows)
             done = o_buf.at[block_rows, :]
             target = out.at[:, pl.ds(pl.multiple_of(head * HD, HD), HD)]
@@ -244,10 +262,10 @@
 
             return inner
 
-        lax.fori_loop(0, NZ, give, 0)
+        lax.fori_loop(0, per_block, give, 0)
         return carry
 
-    lax.fori_loop(0, NY, attend, 0)
+    lax.fori_loop(0, NY * per_chunk, attend, 0)
 
     landed(out, recv_o)
     remote = (NY * NZ - 1) * HD
@@ -268,35 +286,37 @@
         def _():
             landed(buf.at[0], send_shift.at[3 * which + 1])
 
-        @pl.when((core == 0) & behind)
-        def _():
-            landed(buf.at[1], send_shift.at[3 * which + 2])
+        @pl.when((core == 1) & ahead)
+        def _():
+            landed(buf.at[0], send_shift.at[3 * which + 2])
 
 
 def per_device(queries, keys, values, lengths, span_mask, levels, level_gain):
     _, rows, width = queries.shape
     slots = rows * NY * NZ
     hbm = pl.BlockSpec(memory_space=pl.ANY)
-    smem = pl.BlockSpec(memory_space=pltpu.SMEM)
     dma = pltpu.SemaphoreType.DMA
     result = pl.pallas_call(
         attend_kernel,
-        out_shape=jax.ShapeDtypeStruct((rows, width), jnp.bfloat16),
-        in_specs=[smem, smem, smem, hbm, hbm, hbm, hbm],
+        out_shape=pltpu.VMEM((rows, width), jnp.bfloat16),
+        in_specs=[hbm] * 7,
         out_specs=pl.BlockSpec(memory_space=pl.ANY),
         scratch_shapes=[
+            pltpu.SMEM(lengths.shape, jnp.int32),
+            pltpu.SMEM(span_mask.shape[::-1], jnp.int32),
+            pltpu.SMEM(levels.shape, jnp.int32),
             pltpu.VMEM((slots, HD), jnp.bfloat16),
             pltpu.VMEM((WIN + 1, slots, HD), jnp.bfloat16),
             pltpu.VMEM((WIN + 1, slots, HD), jnp.bfloat16),
             pltpu.VMEM((slots, HD), jnp.bfloat16),
             pltpu.VMEM((level_gain.shape[0], HD), jnp.float32),
             dma, dma, dma, dma, dma((6,)),
-            dma((WIN + 1,)), dma((WIN + 1,)), dma((NY,)), dma, dma,
+            dma((WIN + 1,)), dma((WIN + 1,)), dma((NY,)), dma, dma, dma((3,)),
         ],
         compiler_params=pltpu.CompilerParams(
             collective_id=0, has_side_effects=True, vmem_limit_bytes=60 * 1024 * 1024
         ),
-    )(lengths, span_mask, levels, queries[0], keys[0], values[0], level_gain)
+    )(lengths, span_mask.T, levels, queries[0], keys[0], values[0], level_gain)
     return result[None]
 
 

time: 76.5 us -> 72.4 us (0.946)
  the two profiles are of different devices: /device:TPU:8 before, /device:TPU:25 now
where the time goes in v3:
time: 72.4 us; the launch traced here: 71.2 us
  Pallas kernels  70.4 us (97%)
    pallas_call x1, Pallas kernels, per_device(): pl.pallas_call(attend_kernel, out_shape=pltpu.VMEM((rows, width), jnp.bfl...  70.4 us

profile of v3, /device:TPU:25, one launch (start us, length us, event | category | flops | bytes accessed | tf_op | source)
XLA Modules:
  0.0 71.2 jit_solution(3920802695794672482)
XLA Ops:
  0.0 70.4 %shard_map.73 = bf16[32,4096]{1,0:T(8,128)(2,1)S(1)} custom-call(s32[16]{0:T(128)} %lengths_in.1, s32[2,16]{1,0:T(2,128)} %bitcast.9, s32[16]{0:T(128)} %levels_in.1, bf16[32,4096]{1,0:T(8,128)(2,1)} %bitcast.6, bf16[32,4096]{1,0:T(8,128)(2,1)} %bitcast.7, bf16[32,4096]{1,0:T(8,128)(2,1)} %bitcast.8, f32[16,4096]{1,0:T(8,128)} %gain_in.1), custom_call_target="tpu_custom_call" | custom-call | tf_op jit(solution)/shard_map/pallas_call | solution.py:299
  70.4 0.7 copy.9

commit v4 on v3

--- a/solution.py
+++ b/solution.py
@@ -24,7 +24,7 @@
 def attend_kernel(
     lengths_in, mask_in, levels_in, q_in, k_in, v_in, gain_in, out,
     lengths, span_mask, levels,
-    q_buf, k_buf, v_buf, o_buf, gain_buf,
+    q_buf, k_buf, v_buf, o_buf, s_buf, gain_buf,
     send_k, send_v, send_q, send_o, send_shift,
     recv_k, recv_v, recv_q, recv_o, gain_sem, scalar_sem,
 ):
@@ -59,6 +59,41 @@
     def before(cc):
         return beside(lax.rem(group + 2 * NX - 1, 2 * NX), cc)
 
+    barrier = pltpu.get_barrier_semaphore()
+
+    run = lax.rem(group, 2)
+    far = z_lo + jnp.where(run == z_hi, NZ // 2, 0) + NZ
+
+    def token_slot(index):
+        away = ((index + 1) // 2) * (2 * lax.rem(index, 2) - 1)
+        return lax.rem(far + away, NZ)
+
+    token_span = (group // 2) * 4 + run * 2 + core
+    for index in range(NZ):
+        away = ((index + 1) // 2) * (2 * (index % 2) - 1)
+        zz = jnp.bitwise_and(far + away, NZ - 1)
+        for yy in range(NY):
+            place = zz + yy * NZ
+
+            @pl.when(jnp.logical_not(stays & (place == member)))
+            def _():
+                pl.semaphore_signal(
+                    barrier, inc=1, device_id=(token_span, place), device_id_type=MESH
+                )
+
+    @pl.when((core == 0) & jnp.logical_not(first))
+    def _():
+        for cc in range(CORES):
+            pl.semaphore_signal(barrier, inc=1, device_id=before(cc), device_id_type=MESH)
+
+    @pl.when((core == 1) & jnp.logical_not(first))
+    def _():
+        pl.semaphore_signal(barrier, inc=1, device_id=before(1), device_id_type=MESH)
+
+    @pl.when(core == 1)
+    def _():
+        pl.semaphore_signal(barrier, inc=1, device_id=beside(group, 0), device_id_type=MESH)
+
     scalar_copies = [
         pltpu.make_async_copy(source, held, scalar_sem.at[index])
         for index, (source, held) in enumerate(
@@ -67,41 +102,6 @@
     ]
     for copy in scalar_copies:
         copy.start()
-    barrier = pltpu.get_barrier_semaphore()
-
-    run = lax.rem(group, 2)
-    far = z_lo + jnp.where(run == z_hi, NZ // 2, 0) + NZ
-
-    def token_slot(index):
-        away = ((index + 1) // 2) * (2 * lax.rem(index, 2) - 1)
-        return lax.rem(far + away, NZ)
-
-    def greet(index, carry):
-        yy, zz = lax.rem(index, NY), token_slot(index // NY)
-
-        @pl.when(jnp.logical_not(stays & (yy == y) & (zz == z_lo)))
-        def _():
-            pl.semaphore_signal(
-                barrier, inc=1, device_id=token_place(yy, zz), device_id_type=MESH
-            )
-
-        return carry
-
-    lax.fori_loop(0, NY * NZ, greet, 0)
-
-    @pl.when((core == 0) & jnp.logical_not(first))
-    def _():
-        for cc in range(CORES):
-            pl.semaphore_signal(barrier, inc=1, device_id=before(cc), device_id_type=MESH)
-
-    @pl.when((core == 1) & jnp.logical_not(first))
-    def _():
-        pl.semaphore_signal(barrier, inc=1, device_id=before(1), device_id_type=MESH)
-
-    @pl.when(core == 1)
-    def _():
-        pl.semaphore_signal(barrier, inc=1, device_id=beside(group, 0), device_id_type=MESH)
-
     gain_copy = pltpu.make_async_copy(
         gain_in.at[:, pl.ds(pl.multiple_of(head * HD, HD), HD)], gain_buf, gain_sem
     )
@@ -142,6 +142,11 @@
     exchange(v_in, v_buf.at[0], send_v, recv_v.at[0])
     exchange(q_in, q_buf, send_q, recv_q.at[y], (0,))
 
+    @pl.when(lax.rem(y, 2) == 0)
+    def _():
+        exchange(q_in, q_buf, send_q, recv_q.at[y], (1,))
+
+
     def landed(ref, sem):
         pltpu.make_async_copy(ref, ref, sem).wait()
 
@@ -167,18 +172,21 @@
 
         @pl.when(core == 0)
         def _():
+            shift(buf, 0, 1, send_shift.at[3 * which + 1], recv, beside(group, 1)).start()
+
             @pl.when(ahead)
             def _():
                 shift(buf, 0, 2, send_shift.at[3 * which], recv, after(0)).start()
-
-            shift(buf, 0, 1, send_shift.at[3 * which + 1], recv, beside(group, 1)).start()
 
         @pl.when((core == 1) & ahead)
         def _():
             shift(buf, 0, 1, send_shift.at[3 * which], recv, after(0)).start()
             shift(buf, 0, 2, send_shift.at[3 * which + 2], recv, after(1)).start()
 
-    exchange(q_in, q_buf, send_q, recv_q.at[y], (1,))
+    @pl.when(lax.rem(y, 2) == 1)
+    def _():
+        exchange(q_in, q_buf, send_q, recv_q.at[y], (1,))
+
     behind = jnp.logical_not(first)
     for copy in scalar_copies:
         copy.wait()
@@ -207,42 +215,41 @@
         def _():
             landed(buf.at[1], recv.at[1])
 
-    per_chunk = chunk // QB
     per_block = QB // rows
 
-    def attend(index, carry):
-        turn, part = index // per_chunk, lax.rem(index, per_chunk)
+    def attend(turn, carry):
         yy = lax.rem(y - lax.rem(y, 2) + turn, NY)
         base = pl.multiple_of(yy * chunk, chunk)
-
-        @pl.when(part == 0)
-        def _():
-            landed(q_buf.at[pl.ds(base, chunk), :], recv_q.at[yy])
-
-        first_slot = lax.rem(part + far // per_block, per_chunk) * per_block
-        spot = pl.ds(pl.multiple_of(base + first_slot * rows, QB), QB)
-        queries = q_buf[spot, :]
-        scores = []
-        for step in range(WIN + 1):
-            part_scores = lax.dot_general(
-                queries, k_buf[step], (((1,), (1,)), ((), ())), preferred_element_type=jnp.float32
+        landed(q_buf.at[pl.ds(base, chunk), :], recv_q.at[yy])
+        slot = lax.rem(far // per_block, 2) * per_block
+        blocks = (slot, per_block - slot)
+
+        def spot_of(first_slot):
+            return pl.ds(pl.multiple_of(base + first_slot * rows, QB), QB)
+
+        def score(first_slot, step):
+            part = lax.dot_general(
+                q_buf[spot_of(first_slot), :], k_buf[step], (((1,), (1,)), ((), ())),
+                preferred_element_type=jnp.float32,
             )
             live = lax.broadcasted_iota(jnp.int32, (1, slots), 1) < limits[step]
-            scores.append(jnp.where(live, part_scores, NEG))
-        top = functools.reduce(
-            jnp.maximum, [jnp.max(part_scores, axis=-1, keepdims=True) for part_scores in scores]
-        )
-        total = jnp.zeros((QB, 1), jnp.float32)
-        mixed = jnp.zeros((QB, HD), jnp.float32)
-        for step in range(WIN + 1):
-            expd = jnp.exp2((scores[step] - top) * scale)
-            total += jnp.sum(expd, axis=-1, keepdims=True)
-            mixed += jnp.dot(
-                expd.astype(jnp.bfloat16), v_buf[step], preferred_element_type=jnp.float32
+            return jnp.where(live, part, NEG)
+
+        def finish(first_slot, scores):
+            top = functools.reduce(
+                jnp.maximum, [jnp.max(part, axis=-1, keepdims=True) for part in scores]
             )
-        o_buf[spot, :] = (mixed / total * gain_row).astype(jnp.bfloat16)
-
-        def give(offset, inner):
+            total = jnp.zeros((QB, 1), jnp.float32)
+            mixed = jnp.zeros((QB, HD), jnp.float32)
+            for step in range(WIN + 1):
+                expd = jnp.exp2((scores[step] - top) * scale)
+                total += jnp.sum(expd, axis=-1, keepdims=True)
+                mixed += jnp.dot(
+                    expd.astype(jnp.bfloat16), v_buf[step], preferred_element_type=jnp.float32
+                )
+            o_buf[spot_of(first_slot), :] = (mixed / total * gain_row).astype(jnp.bfloat16)
+
+        def give(offset, first_slot):
             zz = first_slot + lax.rem(far + offset, per_block)
             block_rows = pl.ds(pl.multiple_of(base + zz * rows, rows), rows)
             done = o_buf.at[block_rows, :]
@@ -260,12 +267,18 @@
                     device_id=token_place(yy, zz), device_id_type=MESH,
                 ).start()
 
-            return inner
-
-        lax.fori_loop(0, per_block, give, 0)
+            return first_slot
+
+        scores = [score(blocks[0], step) for step in range(WIN + 1)]
+        for step in range(WIN + 1):
+            s_buf[step] = score(blocks[1], step)
+        finish(blocks[0], scores)
+        lax.fori_loop(0, per_block, give, blocks[0])
+        finish(blocks[1], [s_buf[step] for step in range(WIN + 1)])
+        lax.fori_loop(0, per_block, give, blocks[1])
         return carry
 
-    lax.fori_loop(0, NY * per_chunk, attend, 0)
+    lax.fori_loop(0, NY, attend, 0)
 
     landed(out, recv_o)
     remote = (NY * NZ - 1) * HD
@@ -309,6 +322,7 @@
             pltpu.VMEM((WIN + 1, slots, HD), jnp.bfloat16),
             pltpu.VMEM((WIN + 1, slots, HD), jnp.bfloat16),
             pltpu.VMEM((slots, HD), jnp.bfloat16),
+            pltpu.VMEM((WIN + 1, QB, slots), jnp.float32),
             pltpu.VMEM((level_gain.shape[0], HD), jnp.float32),
             dma, dma, dma, dma, dma((6,)),
             dma((WIN + 1,)), dma((WIN + 1,)), dma((NY,)), dma, dma, dma((3,)),

time: 72.4 us -> 71.9 us (level)
  no operation moved by 1% of the time
where the time goes in v4:
time: 71.9 us; the launch traced here: 71.2 us
  Pallas kernels  70.5 us (98%)
    pallas_call x1, Pallas kernels, per_device(): pl.pallas_call(attend_kernel, out_shape=pltpu.VMEM((rows, width), jnp.bfl...  70.5 us

profile of v4, /device:TPU:25, one launch (start us, length us, event | category | flops | bytes accessed | tf_op | source)
XLA Modules:
  0.0 71.2 jit_solution(6775901255817583499)
XLA Ops:
  0.0 70.5 %shard_map.73 = bf16[32,4096]{1,0:T(8,128)(2,1)S(1)} custom-call(s32[16]{0:T(128)} %lengths_in.1, s32[2,16]{1,0:T(2,128)} %bitcast.9, s32[16]{0:T(128)} %levels_in.1, bf16[32,4096]{1,0:T(8,128)(2,1)} %bitcast.6, bf16[32,4096]{1,0:T(8,128)(2,1)} %bitcast.7, bf16[32,4096]{1,0:T(8,128)(2,1)} %bitcast.8, f32[16,4096]{1,0:T(8,128)} %gain_in.1), custom_call_target="tpu_custom_call" | custom-call | tf_op jit(solution)/shard_map/pallas_call | solution.py:312
  70.5 0.7 copy.9

commit v5 on v4

--- a/solution.py
+++ b/solution.py
@@ -111,10 +111,10 @@
         barrier, NY * NZ + 2 - jnp.where(stays, 1, 0) - jnp.where(last, 1 + core, 0)
     )
 
-    def exchange(source, landing, send_sem, recv_sem, turns=(0, 1)):
+    def exchange(source, landing, send_sem, recv_sem, turns=(0, 1), swap=False):
         def step(index, carry):
             turn, place = index // (2 * NZ), 2 * NZ - 1 - lax.rem(index, 2 * NZ)
-            half = lax.rem(y // 2 + turn, 2)
+            half = lax.rem(y // 2 + turn + (1 if swap else 0), 2)
             away = ((place + 1) // 2) * (2 * lax.rem(place, 2) - 1)
             zz = lax.rem(z + away + 2 * NZ, 2 * NZ)
             yy = 2 * half + lax.rem(home // NX + core, 2)
@@ -138,8 +138,8 @@
 
         lax.fori_loop(2 * NZ * turns[0], 2 * NZ * (turns[-1] + 1), step, 0)
 
-    exchange(k_in, k_buf.at[0], send_k, recv_k.at[0])
-    exchange(v_in, v_buf.at[0], send_v, recv_v.at[0])
+    exchange(k_in, k_buf.at[0], send_k, recv_k.at[0], swap=True)
+    exchange(v_in, v_buf.at[0], send_v, recv_v.at[0], swap=True)
     exchange(q_in, q_buf, send_q, recv_q.at[y], (0,))
 
     @pl.when(lax.rem(y, 2) == 0)

time: 71.9 us -> 71.5 us (level)
  no operation moved by 1% of the time
where the time goes in v5:
time: 71.5 us; the launch traced here: 71.4 us
  Pallas kernels  70.7 us (99%)
    pallas_call x1, Pallas kernels, per_device(): pl.pallas_call(attend_kernel, out_shape=pltpu.VMEM((rows, width), jnp.bfl...  70.7 us

profile of v5, /device:TPU:25, one launch (start us, length us, event | category | flops | bytes accessed | tf_op | source)
XLA Modules:
  0.0 71.4 jit_solution(5733407015021168946)
XLA Ops:
  0.0 70.7 %shard_map.73 = bf16[32,4096]{1,0:T(8,128)(2,1)S(1)} custom-call(s32[16]{0:T(128)} %lengths_in.1, s32[2,16]{1,0:T(2,128)} %bitcast.9, s32[16]{0:T(128)} %levels_in.1, bf16[32,4096]{1,0:T(8,128)(2,1)} %bitcast.6, bf16[32,4096]{1,0:T(8,128)(2,1)} %bitcast.7, bf16[32,4096]{1,0:T(8,128)(2,1)} %bitcast.8, f32[16,4096]{1,0:T(8,128)} %gain_in.1), custom_call_target="tpu_custom_call" | custom-call | tf_op jit(solution)/shard_map/pallas_call | solution.py:312
  70.7 0.7 copy.9

commit v6 on v5

--- a/solution.py
+++ b/solution.py
@@ -13,7 +13,7 @@
 CORES = 2
 QB = 128
 MESH = pl.DeviceIdType.MESH
-NEG = -1e30
+NEG = -3e38
 LOG2E = 1.4426950408889634
 
 

time: 71.5 us -> 71.5 us (level)
  no operation moved by 1% of the time
where the time goes in v6:
time: 71.5 us; the launch traced here: 71.4 us
  Pallas kernels  70.7 us (99%)
    pallas_call x1, Pallas kernels, per_device(): pl.pallas_call(attend_kernel, out_shape=pltpu.VMEM((rows, width), jnp.bfl...  70.7 us

profile of v6, /device:TPU:25, one launch (start us, length us, event | category | flops | bytes accessed | tf_op | source)
XLA Modules:
  0.0 71.4 jit_solution(3098667964786823988)
XLA Ops:
  0.0 70.7 %shard_map.73 = bf16[32,4096]{1,0:T(8,128)(2,1)S(1)} custom-call(s32[16]{0:T(128)} %lengths_in.1, s32[2,16]{1,0:T(2,128)} %bitcast.9, s32[16]{0:T(128)} %levels_in.1, bf16[32,4096]{1,0:T(8,128)(2,1)} %bitcast.6, bf16[32,4096]{1,0:T(8,128)(2,1)} %bitcast.7, bf16[32,4096]{1,0:T(8,128)(2,1)} %bitcast.8, f32[16,4096]{1,0:T(8,128)} %gain_in.1), custom_call_target="tpu_custom_call" | custom-call | tf_op jit(solution)/shard_map/pallas_call | solution.py:312
  70.7 0.7 copy.9
